TPU v7x, 256 devices: a whole 4x4x8 slice. The times are simulated.
256 devices in a mesh: grp: 2 (over core), seq: 32 (over z, y), rep: 4 (over x).
Axes of the slice: x: 4, y: 4, z: 8, core: 2. Of those that a mesh axis runs over, the one named last changes fastest.
Arguments:
- qkv: bfloat16 [2, 16384, 3, 4096], P('grp', ('rep', 'seq')), parts along dimension 1, may hold values from -40 to 40
- hidden: bfloat16 [2, 16384, 4096], P('grp', ('rep', 'seq')), parts along dimension 1, may hold values from -6 to 6
- row_map: int32 [16384], P('rep'), parts along dimension 0, may hold values from 0 to 4095, as said below
- frame_flags: int32 [16], P('rep'), parts along dimension 0, may hold values from 0 to 1, as said below
Outputs:
- block_outputs: bfloat16 [2, 16384, 4096], P('grp', ('rep', 'seq')), parts along dimension 1
There are 4 independent parts, one for each index of `rep`. A program takes and returns all parts, laid end to end along the dimension named above; each array names one. Nothing has to cross between parts.
Inputs may be any that keep to these rules, and one draw needn't show every extreme that they name: The context block holds the window frame-alternated: every token t with the same t mod 32 lies on one context device (which device holds which residue class varies by prompt), in a rotated order within the device. So row_map is a permutation, and each run of 128 context rows that one device holds sends exactly 4 rows into each run of 128 main rows that one device holds. `frame_flags`: exactly half of the frames are 1.
All inputs are finite; a program needn't handle non-finite values.
Results may differ from a plain program's by a relative error of at most 0.0031.
Values may be sent and summed in bfloat16 or wider, within the bound.
A program may use at most 64 MiB of HBM per device.

v0:
```python
import math

import jax
import jax.numpy as jnp
from jax import lax
from jax.experimental import pallas as pl
from jax.experimental.pallas import tpu as pltpu
from jax.sharding import PartitionSpec as P

HEAD = 128
ROWS = 128
PEERS = 32
ZS = 8
YS = 4
TOKENS = ROWS * PEERS
FRAMES = 4
PAIR = 2
BLOCK = PAIR * ROWS
CHUNK = 512
LEAD = 14
HELD = 10
LEAD_SENT, K_SENT, V_SENT, Q_SENT, BACK_SENT, HINT_SENT, K_GOT, V_GOT, HINT_GOT = range(9)
SCALE = HEAD ** -0.5 * math.log2(math.e)
MESH = pl.DeviceIdType.MESH
LAST_DIMS = (((1,), (1,)), ((), ()))


def offset(step):
    turn = lax.rem(step, ZS)
    dz = jnp.where(lax.rem(turn, 2) == 1, ZS - (turn + 1) // 2, turn // 2)
    return dz, step // ZS


def ahead(me, step):
    dz, dy = offset(step)
    return lax.rem(me // YS + dz, ZS) * YS + lax.rem(lax.rem(me, YS) + dy, YS)


def behind(me, step):
    dz, dy = offset(step)
    return lax.rem(me // YS + ZS - dz, ZS) * YS + lax.rem(lax.rem(me, YS) + YS - dy, YS)


def columns(peer):
    return pl.ds(pl.multiple_of(peer * HEAD, HEAD), HEAD)


def score(queries, keys, scores, peak):
    highest = jnp.full((BLOCK, 128), -jnp.inf, jnp.float32)
    for start in range(0, TOKENS, CHUNK):
        part = lax.dot_general(
            queries, keys[pl.ds(start, CHUNK), :], LAST_DIMS, preferred_element_type=jnp.float32
        )
        scores[:, pl.ds(start, CHUNK)] = part
        for lane in range(0, CHUNK, 128):
            highest = jnp.maximum(highest, part[:, lane:lane + 128])
    peak[...] = jnp.broadcast_to(jnp.max(highest, axis=1, keepdims=True), (BLOCK, 128))


def blend(values, scores, peak, queries=None, keys=None, next_scores=None):
    level = peak[...]
    totals = jnp.zeros((BLOCK, 128), jnp.float32)
    blended = jnp.zeros((BLOCK, HEAD), jnp.float32)
    highest = jnp.full((BLOCK, 128), -jnp.inf, jnp.float32)
    for start in range(0, TOKENS, CHUNK):
        if queries is not None:
            part = lax.dot_general(
                queries, keys[pl.ds(start, CHUNK), :], LAST_DIMS, preferred_element_type=jnp.float32
            )
        rounded = []
        for lane in range(0, CHUNK, 128):
            weights = jnp.exp2((scores[:, pl.ds(start + lane, 128)] - level) * SCALE)
            totals = totals + weights
            rounded.append(weights.astype(jnp.bfloat16))
        if queries is not None:
            next_scores[:, pl.ds(start, CHUNK)] = part
            for lane in range(0, CHUNK, 128):
                highest = jnp.maximum(highest, part[:, lane:lane + 128])
        blended = blended + jnp.dot(
            jnp.concatenate(rounded, axis=1),
            values[pl.ds(start, CHUNK), :],
            preferred_element_type=jnp.float32,
        )
    if queries is not None:
        peak[...] = jnp.broadcast_to(jnp.max(highest, axis=1, keepdims=True), (BLOCK, 128))
    return (blended / jnp.sum(totals, axis=1, keepdims=True)).astype(jnp.bfloat16)


def kernel(
    qkv, hidden, row_map, frame_flags, out,
    keys, values, queries, even, odd, peak, attended, ordered, hint, placed, landed, stream,
    flags, map_rows, map_cells, owner_of, slot_of,
    bulk, q_got, back_got, local_sem, turn,
):
    grp = lax.axis_index("grp")
    me = lax.axis_index("seq")

    def push(src, dst, sent, got, **device):
        return pltpu.make_async_remote_copy(
            src_ref=src, dst_ref=dst, send_sem=bulk.at[sent], recv_sem=got,
            device_id=device, device_id_type=MESH,
        )

    def key_copy(step, sent):
        peer = ahead(me, step)
        return push(qkv.at[1, :, columns(peer)], keys.at[step], sent, bulk.at[K_GOT], seq=peer)

    def value_copy(step):
        peer = ahead(me, step)
        return push(qkv.at[2, :, columns(peer)], values.at[step], V_SENT, bulk.at[V_GOT], seq=peer)

    def query_copy(step):
        peer = ahead(me, step)
        return push(
            qkv.at[0, :, columns(peer)], queries.at[step], Q_SENT, q_got.at[step // PAIR], seq=peer
        )

    def back_copy(step):
        return push(
            attended.at[step], landed.at[step], BACK_SENT, back_got.at[step // PAIR], seq=behind(me, step)
        )

    def hint_copy(step):
        return push(ordered.at[step], hint.at[step], HINT_SENT, bulk.at[HINT_GOT], grp=1 - grp)

    def whole(ref, first, count, sent, got):
        part = ref.at[pl.ds(first, count)]
        return push(part, part, sent, got, seq=ahead(me, 1))

    def each(first, last, body):
        def step(i, carry):
            body(i)
            return carry
        lax.fori_loop(first, last, step, 0)

    own = [
        pltpu.make_async_copy(qkv.at[1, :, columns(me)], keys.at[0], local_sem.at[0]),
        pltpu.make_async_copy(qkv.at[2, :, columns(me)], values.at[0], local_sem.at[1]),
        pltpu.make_async_copy(qkv.at[0, :, columns(me)], queries.at[0], local_sem.at[2]),
        pltpu.make_async_copy(hidden, stream, local_sem.at[3]),
        pltpu.make_async_copy(row_map, map_rows, local_sem.at[4]),
        pltpu.make_async_copy(row_map, map_cells, local_sem.at[5]),
        pltpu.make_async_copy(frame_flags, flags, local_sem.at[6]),
    ]
    barrier = pltpu.get_barrier_semaphore()
    each(1, PEERS, lambda i: pl.semaphore_signal(
        barrier, inc=1, device_id={"seq": ahead(me, i)}, device_id_type=MESH))
    pl.semaphore_signal(barrier, inc=1, device_id={"grp": 1 - grp}, device_id_type=MESH)
    pl.semaphore_wait(barrier, PEERS)

    def send_keys_values():
        each(1, 1 + LEAD, lambda i: key_copy(i, LEAD_SENT).start())
        each(1 + LEAD, PEERS, lambda i: key_copy(i, K_SENT).start())
        each(1, PEERS, lambda i: value_copy(i).start())

    @pl.when(grp == 0)
    def _():
        send_keys_values()
        for copy in own:
            copy.start()

        def find(residue):
            def look(c, found):
                return jnp.where(lax.rem(map_cells[c, 0], PEERS) == residue, c, found)
            source = lax.fori_loop(0, PEERS, look, 0)
            dz = lax.rem(me // YS + ZS - source // YS, ZS)
            dy = lax.rem(lax.rem(me, YS) + YS - lax.rem(source, YS), YS)
            owner_of[residue] = source
            slot_of[residue] = dy * ZS + jnp.where(dz < ZS // 2, 2 * dz, 2 * ZS - 1 - 2 * dz)

        whole(keys, 1, LEAD, LEAD_SENT, bulk.at[K_GOT]).wait_send()
        pl.semaphore_signal(turn, inc=1, device_id={"grp": 1}, device_id_type=MESH)
        own[5].wait()
        each(0, PEERS, find)

    @pl.when(grp == 1)
    def _():
        for copy in own:
            copy.start()
        pl.semaphore_wait(turn, 1)
        send_keys_values()
        whole(keys, 1, LEAD, LEAD_SENT, bulk.at[K_GOT]).wait_send()
        own[5].wait()

    whole(keys, 1 + LEAD, PEERS - 1 - LEAD, K_SENT, bulk.at[K_GOT]).wait_send()
    whole(values, 1, PEERS - 1, V_SENT, bulk.at[V_GOT]).wait_send()
    each(1, PEERS, lambda i: query_copy(i).start())
    for copy in own[:5] + own[6:]:
        copy.wait()
    whole(keys, 1, PEERS - 1, K_SENT, bulk.at[K_GOT]).wait_recv()
    whole(values, 1, PEERS - 1, V_SENT, bulk.at[V_GOT]).wait_recv()

    flat_keys = keys.reshape(TOKENS, HEAD)
    flat_values = values.reshape(TOKENS, HEAD)
    blocks = PEERS // PAIR

    def query_rows(block):
        whole(queries, block * PAIR, PAIR, Q_SENT, q_got.at[block]).wait_recv()
        return queries[pl.ds(block * PAIR, PAIR)].reshape(BLOCK, HEAD)

    def give_back(step):
        @pl.when(step > 0)
        def _():
            back_copy(step).start()

    def add_hint(step):
        token_peer = behind(me, step)
        gate = flags[token_peer // (PEERS // FRAMES)].astype(jnp.float32)
        total = attended[step].astype(jnp.float32) + gate * hint[step].astype(jnp.float32)
        attended[step] = total.astype(jnp.bfloat16)
        give_back(step)

    def deliver(block, result):
        first = block * PAIR
        attended[pl.ds(first, PAIR)] = result.reshape(PAIR, ROWS, HEAD)

        @pl.when(grp == 0)
        def _():
            for step in (first, first + 1):
                give_back(step)

        @pl.when(jnp.logical_and(grp == 1, block + 1 == HELD))
        def _():
            whole(hint, 0, PEERS, HINT_SENT, bulk.at[HINT_GOT]).wait_recv()
            each(0, HELD * PAIR, add_hint)

        @pl.when(jnp.logical_and(grp == 1, block + 1 > HELD))
        def _():
            for step in (first, first + 1):
                add_hint(step)

    def work(block):
        rows = query_rows(block + 1)

        @pl.when(lax.rem(block, 2) == 0)
        def _():
            deliver(block, blend(flat_values, even, peak, rows, flat_keys, odd))

        @pl.when(lax.rem(block, 2) == 1)
        def _():
            deliver(block, blend(flat_values, odd, peak, rows, flat_keys, even))

    whole(queries, 1, PAIR - 1, Q_SENT, q_got.at[0]).wait_recv()
    score(queries[pl.ds(0, PAIR)].reshape(BLOCK, HEAD), flat_keys, even, peak)
    each(0, blocks - 1, work)
    deliver(blocks - 1, blend(flat_values, odd, peak))

    @pl.when(grp == 0)
    def _():
        def place(residue, carry):
            source = owner_of[residue]
            spots = map_rows[pl.ds(source, 1), :] // PEERS
            chosen = lax.broadcasted_iota(jnp.int32, (ROWS, ROWS), 0) == spots
            rows = jnp.dot(
                chosen.astype(jnp.bfloat16),
                attended[slot_of[residue]],
                preferred_element_type=jnp.float32,
            )
            placed[pl.ds(residue, ROWS, stride=PEERS), :] = rows
            return carry
        lax.fori_loop(0, PEERS, place, 0, unroll=8)

        def hand_over(step):
            token_peer = behind(me, step)
            rows = placed[pl.ds(pl.multiple_of(token_peer * ROWS, ROWS), ROWS), :]
            ordered[step] = rows.astype(jnp.bfloat16)
            hint_copy(step).start()
        each(0, PEERS, hand_over)

    whole(queries, 1, PEERS - 1, Q_SENT, q_got.at[0]).wait_send()

    def finish(step, rows):
        cols = columns(ahead(me, step))
        total = stream[:, cols].astype(jnp.float32) + rows.astype(jnp.float32)
        out[:, cols] = total.astype(jnp.bfloat16)

    finish(0, attended[0])
    whole(landed, 1, PAIR - 1, BACK_SENT, back_got.at[0]).wait_recv()
    each(1, PAIR, lambda i: finish(i, landed[i]))

    def finish_block(block):
        whole(landed, block * PAIR, PAIR, BACK_SENT, back_got.at[block]).wait_recv()
        for step in (block * PAIR, block * PAIR + 1):
            finish(step, landed[step])
    each(1, blocks, finish_block)

    whole(attended, 1, PEERS - 1, BACK_SENT, back_got.at[0]).wait_send()

    @pl.when(grp == 0)
    def _():
        whole(ordered, 0, PEERS, HINT_SENT, bulk.at[HINT_GOT]).wait_send()


def local(qkv, hidden, row_map, frame_flags):
    planes = jnp.transpose(qkv[0], (1, 0, 2))
    cells = row_map.reshape(PEERS, ROWS)
    wide = PEERS * HEAD
    pairs = PEERS * TOKENS * HEAD * ROWS
    result = pl.pallas_call(
        kernel,
        out_shape=pltpu.VMEM((ROWS, wide), jnp.bfloat16),
        in_specs=[
            pl.BlockSpec(memory_space=pl.ANY),
            pl.BlockSpec(memory_space=pl.ANY),
            pl.BlockSpec(memory_space=pl.ANY),
            pl.BlockSpec(memory_space=pl.ANY),
        ],
        out_specs=pl.BlockSpec(memory_space=pltpu.VMEM),
        scratch_shapes=[
            pltpu.VMEM((PEERS, ROWS, HEAD), jnp.bfloat16),
            pltpu.VMEM((PEERS, ROWS, HEAD), jnp.bfloat16),
            pltpu.VMEM((PEERS, ROWS, HEAD), jnp.bfloat16),
            pltpu.VMEM((BLOCK, TOKENS), jnp.float32),
            pltpu.VMEM((BLOCK, TOKENS), jnp.float32),
            pltpu.VMEM((BLOCK, 128), jnp.float32),
            pltpu.VMEM((PEERS, ROWS, HEAD), jnp.bfloat16),
            pltpu.VMEM((PEERS, ROWS, HEAD), jnp.bfloat16),
            pltpu.VMEM((PEERS, ROWS, HEAD), jnp.bfloat16),
            pltpu.VMEM((TOKENS + PEERS, HEAD), jnp.float32),
            pltpu.VMEM((PEERS, ROWS, HEAD), jnp.bfloat16),
            pltpu.VMEM((ROWS, wide), jnp.bfloat16),
            pltpu.SMEM((FRAMES,), jnp.int32),
            pltpu.VMEM((PEERS, ROWS), jnp.int32),
            pltpu.SMEM((PEERS, ROWS), jnp.int32),
            pltpu.SMEM((PEERS,), jnp.int32),
            pltpu.SMEM((PEERS,), jnp.int32),
            pltpu.SemaphoreType.DMA((9,)),
            pltpu.SemaphoreType.DMA((PEERS // PAIR,)),
            pltpu.SemaphoreType.DMA((PEERS // PAIR,)),
            pltpu.SemaphoreType.DMA((7,)),
            pltpu.SemaphoreType.REGULAR,
        ],
        compiler_params=pltpu.CompilerParams(
            collective_id=0, has_side_effects=True, vmem_limit_bytes=60 * 1024 * 1024
        ),
        cost_estimate=pl.CostEstimate(
            flops=4 * pairs, bytes_accessed=6 * ROWS * wide * 2, transcendentals=TOKENS * TOKENS
        ),
        name="attend_and_exchange",
    )(planes, hidden[0], cells, frame_flags)
    return result[None]


def solution(mesh):
    in_specs = (
        P("grp", ("rep", "seq"), None, None),
        P("grp", ("rep", "seq"), None),
        P("rep"),
        P("rep"),
    )
    out_specs = P("grp", ("rep", "seq"), None)
    return jax.shard_map(local, mesh=mesh, in_specs=in_specs, out_specs=out_specs, check_vma=False)
```

profile of v0, /device:TPU:1, one launch (start us, length us, event | category | flops | bytes accessed | tf_op | source)
XLA Modules:
  0.0 105.6 jit_solution(280597147100001971)
XLA Ops:
  0.0 104.6 %attend_and_exchange.1 = bf16[128,4096]{1,0:T(8,128)(2,1)S(1)} custom-call(bf16[3,128,4096]{2,1,0:T(8,128)(2,1)} %bitcast.7, bf16[128,4096]{1,0:T(8,128)(2,1)} %bitcast.8, s32[32,128]{1,0:T(8,128)} %bitcast.9, s32[4]{0:T(128)} %frame_flags.1), custom_call_target="tpu_custom_call" | custom-call | flops 8589934592 | bytes 6291456 | tf_op jit(solution)/shard_map/attend_and_exchange/pallas_call | solution.py:299
  104.6 1.0 copy.6
where the time goes:
time: 106 us
  Pallas kernels  105 us (99%)
    pallas_call x1, Pallas kernels, local(): pl.pallas_call(kernel, out_shape=pltpu.VMEM((ROWS, wide), jnp.bfloat16),...  105 us

commit v1 on v0

--- a/solution.py
+++ b/solution.py
@@ -127,11 +127,11 @@
         part = ref.at[pl.ds(first, count)]
         return push(part, part, sent, got, seq=ahead(me, 1))
 
-    def each(first, last, body):
+    def each(first, last, body, unroll=1):
         def step(i, carry):
             body(i)
             return carry
-        lax.fori_loop(first, last, step, 0)
+        lax.fori_loop(first, last, step, 0, unroll=unroll)
 
     own = [
         pltpu.make_async_copy(qkv.at[1, :, columns(me)], keys.at[0], local_sem.at[0]),
@@ -144,14 +144,14 @@
     ]
     barrier = pltpu.get_barrier_semaphore()
     each(1, PEERS, lambda i: pl.semaphore_signal(
-        barrier, inc=1, device_id={"seq": ahead(me, i)}, device_id_type=MESH))
+        barrier, inc=1, device_id={"seq": ahead(me, i)}, device_id_type=MESH), unroll=8)
     pl.semaphore_signal(barrier, inc=1, device_id={"grp": 1 - grp}, device_id_type=MESH)
     pl.semaphore_wait(barrier, PEERS)
 
     def send_keys_values():
-        each(1, 1 + LEAD, lambda i: key_copy(i, LEAD_SENT).start())
-        each(1 + LEAD, PEERS, lambda i: key_copy(i, K_SENT).start())
-        each(1, PEERS, lambda i: value_copy(i).start())
+        each(1, 1 + LEAD, lambda i: key_copy(i, LEAD_SENT).start(), unroll=7)
+        each(1 + LEAD, PEERS, lambda i: key_copy(i, K_SENT).start(), unroll=8)
+        each(1, PEERS, lambda i: value_copy(i).start(), unroll=8)
 
     @pl.when(grp == 0)
     def _():
@@ -184,7 +184,7 @@
 
     whole(keys, 1 + LEAD, PEERS - 1 - LEAD, K_SENT, bulk.at[K_GOT]).wait_send()
     whole(values, 1, PEERS - 1, V_SENT, bulk.at[V_GOT]).wait_send()
-    each(1, PEERS, lambda i: query_copy(i).start())
+    each(1, PEERS, lambda i: query_copy(i).start(), unroll=8)
     for copy in own[:5] + own[6:]:
         copy.wait()
     whole(keys, 1, PEERS - 1, K_SENT, bulk.at[K_GOT]).wait_recv()
@@ -222,7 +222,7 @@
         @pl.when(jnp.logical_and(grp == 1, block + 1 == HELD))
         def _():
             whole(hint, 0, PEERS, HINT_SENT, bulk.at[HINT_GOT]).wait_recv()
-            each(0, HELD * PAIR, add_hint)
+            each(0, HELD * PAIR, add_hint, unroll=4)
 
         @pl.when(jnp.logical_and(grp == 1, block + 1 > HELD))
         def _():
@@ -265,7 +265,7 @@
             rows = placed[pl.ds(pl.multiple_of(token_peer * ROWS, ROWS), ROWS), :]
             ordered[step] = rows.astype(jnp.bfloat16)
             hint_copy(step).start()
-        each(0, PEERS, hand_over)
+        each(0, PEERS, hand_over, unroll=8)
 
     whole(queries, 1, PEERS - 1, Q_SENT, q_got.at[0]).wait_send()
 

time: 106 us -> 106 us (level)
  no operation moved by 1% of the time
where the time goes in v1:
time: 106 us; the launch traced here: 105 us
  Pallas kernels  104 us (98%)
    pallas_call x1, Pallas kernels, local(): pl.pallas_call(kernel, out_shape=pltpu.VMEM((ROWS, wide), jnp.bfloat16),...  104 us

profile of v1, /device:TPU:1, one launch (start us, length us, event | category | flops | bytes accessed | tf_op | source)
XLA Modules:
  0.0 105.5 jit_solution(3498978437722974543)
XLA Ops:
  0.0 104.5 %attend_and_exchange.1 = bf16[128,4096]{1,0:T(8,128)(2,1)S(1)} custom-call(bf16[3,128,4096]{2,1,0:T(8,128)(2,1)} %bitcast.7, bf16[128,4096]{1,0:T(8,128)(2,1)} %bitcast.8, s32[32,128]{1,0:T(8,128)} %bitcast.9, s32[4]{0:T(128)} %frame_flags.1), custom_call_target="tpu_custom_call" | custom-call | flops 8589934592 | bytes 6291456 | tf_op jit(solution)/shard_map/attend_and_exchange/pallas_call | solution.py:299
  104.5 1.0 copy.6

commit v2 on v1

--- a/solution.py
+++ b/solution.py
@@ -258,7 +258,7 @@
             )
             placed[pl.ds(residue, ROWS, stride=PEERS), :] = rows
             return carry
-        lax.fori_loop(0, PEERS, place, 0, unroll=8)
+        lax.fori_loop(0, PEERS, place, 0, unroll=16)
 
         def hand_over(step):
             token_peer = behind(me, step)
@@ -282,7 +282,7 @@
         whole(landed, block * PAIR, PAIR, BACK_SENT, back_got.at[block]).wait_recv()
         for step in (block * PAIR, block * PAIR + 1):
             finish(step, landed[step])
-    each(1, blocks, finish_block)
+    each(1, blocks, finish_block, unroll=5)
 
     whole(attended, 1, PEERS - 1, BACK_SENT, back_got.at[0]).wait_send()
 

time: 106 us -> 106 us (level)
  no operation moved by 1% of the time
where the time goes in v2:
time: 106 us; the launch traced here: 105 us
  Pallas kernels  104 us (98%)
    pallas_call x1, Pallas kernels, local(): pl.pallas_call(kernel, out_shape=pltpu.VMEM((ROWS, wide), jnp.bfloat16),...  104 us

profile of v2, /device:TPU:1, one launch (start us, length us, event | category | flops | bytes accessed | tf_op | source)
XLA Modules:
  0.0 105.5 jit_solution(17916409805900316565)
XLA Ops:
  0.0 104.5 %attend_and_exchange.1 = bf16[128,4096]{1,0:T(8,128)(2,1)S(1)} custom-call(bf16[3,128,4096]{2,1,0:T(8,128)(2,1)} %bitcast.7, bf16[128,4096]{1,0:T(8,128)(2,1)} %bitcast.8, s32[32,128]{1,0:T(8,128)} %bitcast.9, s32[4]{0:T(128)} %frame_flags.1), custom_call_target="tpu_custom_call" | custom-call | flops 8589934592 | bytes 6291456 | tf_op jit(solution)/shard_map/attend_and_exchange/pallas_call | solution.py:299
  104.5 1.0 copy.6
